TPU v7x, 32 devices: a whole 2x2x4 slice. The times are simulated.
32 devices in a mesh: groups: 2 (over y), ctx: 16 (over z, x, core).
Axes of the slice: x: 2, y: 2, z: 4, core: 2. Of those that a mesh axis runs over, the one named last changes fastest.
Arguments:
- query_rows: bfloat16 [8192, 4096], P(('groups', 'ctx')), parts along dimension 0, may hold values from -6 to 6
- key_rows: bfloat16 [8192, 4096], P(('groups', 'ctx')), parts along dimension 0, may hold values from -6 to 6
- value_rows: bfloat16 [8192, 4096], P(('groups', 'ctx')), parts along dimension 0, may hold values from -6 to 6
- conv_taps: float32 [2, 4, 4096], replicated, may hold values from -3 to 3
- level_table: float32 [64, 12, 32], replicated, may hold values from 0.2 to 2
- table_index: int32 [8192], P(('groups', 'ctx')), parts along dimension 0, may hold values from 0 to 63
- level_columns: int32 [32, 12], P(('groups', 'ctx')), parts along dimension 0, may hold values from 0 to 11
Outputs:
- attended: bfloat16 [8192, 4096], P(('groups', 'ctx')), parts along dimension 0
There are 2 independent parts, one for each index of `groups`. A program takes and returns all parts, laid end to end along the dimension named above; an argument that names none is the same for every part. Nothing has to cross between parts.
All inputs are finite; a program needn't handle non-finite values.
Results may differ from a plain program's by a relative error of at most 0.0054.
Values may be sent and summed in bfloat16 or wider, within the bound.
A program may use at most 128 MiB of HBM per device.

v0:
```python
import functools
import math

import jax
import jax.numpy as jnp
from jax import lax
from jax.experimental import pallas as pl
from jax.experimental.pallas import tpu as pltpu
from jax.sharding import PartitionSpec as P

F32 = jnp.float32
BF16 = jnp.bfloat16
PAD = 16


def level_factors(levels, block_len, head_dim):
    inv_root = 1.0 / math.sqrt(head_dim)
    factors = [inv_root / math.sqrt(block_len)]
    for level_pos in range(1, levels):
        factors.append(inv_root / math.sqrt(block_len * 2 ** (level_pos - 1)))
    return factors


def kernel(
    bits, heads, dim, q_hbm, k_hbm, v_hbm, taps_ref, table_ref, index_ref, cols_ref,
    out_ref, q_v, k_v, v_v, qc, kc, st_f, st_b, half_f, half_b, quart_f, quart_b,
    buck, acc, coef, load_sem, send_sem, recv_sem,
):
    tokens = q_hbm.shape[0]
    n = 2**bits
    group = lax.axis_index("groups")
    pos = lax.axis_index("ctx")
    bit = [(pos // 2**b) % 2 for b in range(bits)]
    partner = [pos + 2**b * (1 - 2 * bit[b]) for b in range(bits)]
    quarter = heads // 4
    half = heads // 2

    loads = [
        pltpu.make_async_copy(src, dst.at[pl.ds(start, tokens)], load_sem.at[i])
        for i, (src, dst, start) in enumerate(((k_hbm, k_v, PAD), (v_hbm, v_v, 0), (q_hbm, q_v, PAD)))
    ]
    for load in loads:
        load.start()

    barrier = pltpu.get_barrier_semaphore()

    def greet(other):
        pl.semaphore_signal(
            barrier, inc=1, device_id=(group, other), device_id_type=pl.DeviceIdType.MESH
        )

    for b in range(bits):
        greet(partner[b])

    @pl.when(pos > 0)
    def _():
        greet(pos - 1)

    @pl.when(pos < n - 1)
    def _():
        greet(pos + 1)

    ends = (pos == 0).astype(jnp.int32) + (pos == n - 1).astype(jnp.int32)
    pl.semaphore_wait(barrier, bits + 2 - ends)

    def remote(i, src, dst, other):
        return pltpu.make_async_remote_copy(
            src_ref=src, dst_ref=dst, send_sem=send_sem.at[i], recv_sem=recv_sem.at[i],
            device_id=(group, other), device_id_type=pl.DeviceIdType.MESH,
        )

    started = []

    def send(copy, when=None):
        started.append((copy, when))
        if when is None:
            copy.start()
        else:
            pl.when(when)(copy.start)

    def wait(copy, when=None):
        if when is None:
            copy.wait_recv()
        else:
            pl.when(when)(copy.wait_recv)

    rims = []
    for i, (src, dst) in enumerate(((k_hbm, k_v), (q_hbm, q_v))):
        rim = remote(i, src.at[pl.ds(tokens - PAD, PAD)], dst.at[pl.ds(0, PAD)], pos + 1)
        send(rim, pos < n - 1)
        rims.append(rim)

    def finish_rim(i, ref):
        wait(rims[i], pos > 0)

        @pl.when(pos == 0)
        def _():
            ref[pl.ds(0, PAD), :] = jnp.zeros((PAD, ref.shape[1]), BF16)

    def lanes(h):
        return pl.ds(pl.multiple_of(h * dim, dim), dim)

    def conv(ref, which, h):
        rows = ref[:, lanes(h)].astype(F32)
        taps = taps_ref[which, :, lanes(h)]
        count = taps.shape[0]
        total = taps[count - 1 : count] * rows[PAD:]
        for back in range(1, count):
            total = total + taps[count - 1 - back : count - back] * pltpu.roll(rows, back, 0)[PAD:]
        return (0.5 * total * (1.0 + jnp.tanh(0.5 * total))).astype(BF16)

    def state_body(h, carry):
        key = conv(k_v, 1, h)
        kc[h] = key
        state = lax.dot_general(
            key, v_v[:, lanes(h)], (((0,), (0,)), ((), ())), preferred_element_type=F32
        )
        st_f[h] = state
        st_b[h] = state.astype(BF16)
        return carry

    own_half = bit[0] * half
    other_half = (1 - bit[0]) * half
    own_quart = own_half + bit[1] * quarter
    other_quart = own_half + (1 - bit[1]) * quarter

    loads[0].wait()
    loads[1].wait()
    finish_rim(0, k_v)
    firsts = [
        other_half + (1 - bit[1]) * quarter, other_half + bit[1] * quarter, other_quart, own_quart
    ]
    pair = []
    for i, first in enumerate(firsts):
        lax.fori_loop(first, first + quarter, state_body, 0)
        heads_i = pl.ds(first, quarter)
        copy = remote(2 + i, st_b.at[heads_i], buck.at[0, heads_i], partner[0])
        send(copy, None if i < 2 else bit[0] == 0)
        pair.append(copy)

    def coefficients():
        table = table_ref[...]
        rows, levels, _ = table.shape
        factors = level_factors(levels, tokens, dim)
        middle = lax.broadcasted_iota(jnp.int32, table.shape, 1)
        head_id = lax.broadcasted_iota(jnp.int32, (heads, heads * 8), 0)
        lane_id = lax.broadcasted_iota(jnp.int32, (heads, heads * 8), 1)
        mixed = jnp.zeros((rows, heads * 8), F32)
        for level in range(bits + 1):
            column = jnp.sum(jnp.where(middle == cols_ref[0, level], table, 0.0), axis=1)
            place = (lane_id == head_id * 8 + level).astype(F32)
            mixed = mixed + jnp.dot(
                column * factors[level], place,
                precision=lax.Precision.HIGHEST, preferred_element_type=F32,
            )
        hot = (lax.broadcasted_iota(jnp.int32, (rows, tokens), 0) == index_ref[...]).astype(F32)
        weights = jnp.dot(
            hot.T, mixed, precision=lax.Precision.HIGHEST, preferred_element_type=F32
        )
        for h in range(heads):
            coef[h] = weights[:, h * 8 : h * 8 + 8]

    coefficients()

    for i in range(2):
        wait(pair[i])

    def half_body(i, carry):
        h = own_half + i
        total = st_f[h] + buck[0, h].astype(F32)
        half_f[i] = total
        half_b[i] = total.astype(BF16)
        return carry

    lax.fori_loop(0, half, half_body, 0)
    shares = []
    for i, (inner, first) in enumerate((
        ((1 - bit[1]) * quarter, other_quart), (bit[1] * quarter, own_quart)
    )):
        copy = remote(
            6 + i, half_b.at[pl.ds(inner, quarter)], buck.at[1, pl.ds(first, quarter)], partner[1]
        )
        send(copy, None if i == 0 else bit[1] == 0)
        shares.append(copy)

    causal = lax.broadcasted_iota(jnp.int32, (tokens, tokens), 0) >= lax.broadcasted_iota(
        jnp.int32, (tokens, tokens), 1
    )

    def local_body(h, carry):
        query = conv(q_v, 0, h)
        qc[h] = query
        score = lax.dot_general(
            query, kc[h], (((1,), (1,)), ((), ())), preferred_element_type=F32
        )
        score = jnp.where(causal, score, 0.0).astype(BF16)
        read = jnp.dot(score, v_v[:, lanes(h)], preferred_element_type=F32)
        acc[h] = read * coef[h][:, 0:1]
        return carry

    def local(part):
        lax.fori_loop(part * quarter, (part + 1) * quarter, local_body, 0)

    loads[2].wait()
    finish_rim(1, q_v)
    local(0)

    wait(shares[0])

    def quart_body(i, carry):
        total = half_f[bit[1] * quarter + i] + buck[1, own_quart + i].astype(F32)
        quart_f[i] = total
        quart_b[0, i] = total.astype(BF16)
        return carry

    lax.fori_loop(0, quarter, quart_body, 0)
    base = 9

    def exchange(b):
        copy = remote(
            base + 3 * (b - 2), quart_b.at[b - 2], buck.at[b, pl.ds(own_quart, quarter)], partner[b]
        )
        send(copy, None if b < bits - 1 else bit[b] == 0)
        return copy

    hops = {2: exchange(2)}

    wait(shares[1], bit[1] == 1)
    over = remote(
        8, buck.at[1, pl.ds(own_half, half)], buck.at[1, pl.ds(own_half, half)], partner[0]
    )
    send(over, bit[1] == 1)
    local(1)

    def gather_x(b):
        quart = buck.at[b, pl.ds(own_quart, quarter)]
        copy = remote(base + 3 * (b - 2) + 1, quart, quart, partner[1])
        send(copy, bit[b] == 1)
        return copy

    def gather_core(b):
        own = buck.at[b, pl.ds(own_half, half)]
        copy = remote(base + 3 * (b - 2) + 2, own, own, partner[0])
        send(copy, bit[b] == 1)
        return copy

    gx = {}
    gc = {}
    for b in range(2, bits):
        wait(hops[b], None if b < bits - 1 else bit[b] == 1)
        gx[b] = gather_x(b)
        if b < bits - 1:

            def more_body(i, carry, b=b):
                total = quart_f[i] + buck[b, own_quart + i].astype(F32)
                quart_f[i] = total
                quart_b[b - 1, i] = total.astype(BF16)
                return carry

            lax.fori_loop(0, quarter, more_body, 0)
            hops[b + 1] = exchange(b + 1)
        if b == 2:
            local(2)
            local(3)
        wait(gx[b], bit[b] == 1)
        gc[b] = gather_core(b)

    def read_level(b):
        def body(h, carry):
            acc[h] += (
                jnp.dot(qc[h], buck[b, h], preferred_element_type=F32) * coef[h][:, b + 1 : b + 2]
            )
            return carry

        @pl.when(bit[b] == 1)
        def _():
            lax.fori_loop(0, heads, body, 0)

    wait(pair[2], bit[0] == 1)
    wait(pair[3], bit[0] == 1)
    read_level(0)
    wait(over, bit[1] == 1)
    read_level(1)
    for b in range(2, bits):
        wait(gc[b], bit[b] == 1)
        read_level(b)

    def out_body(h, carry):
        out_ref[:, lanes(h)] = acc[h].astype(BF16)
        return carry

    lax.fori_loop(0, heads, out_body, 0)

    for copy, when in started:
        if when is None:
            copy.wait_send()
        else:
            pl.when(when)(copy.wait_send)


def on_device(query_rows, key_rows, value_rows, conv_taps, level_table, table_index, level_columns):
    tokens, width = query_rows.shape
    heads = level_table.shape[2]
    dim = width // heads
    bits = lax.axis_size("ctx").bit_length() - 1
    quarter = heads // 4
    vmem = pl.BlockSpec(memory_space=pltpu.VMEM)
    hbm = pl.BlockSpec(memory_space=pl.ANY)
    copies = 9 + 3 * (bits - 2)
    return pl.pallas_call(
        functools.partial(kernel, bits, heads, dim),
        out_shape=jax.ShapeDtypeStruct((tokens, width), BF16),
        in_specs=[hbm, hbm, hbm, vmem, vmem, vmem, pl.BlockSpec(memory_space=pltpu.SMEM)],
        out_specs=vmem,
        scratch_shapes=[
            pltpu.VMEM((PAD + tokens, width), BF16),
            pltpu.VMEM((PAD + tokens, width), BF16),
            pltpu.VMEM((tokens, width), BF16),
            pltpu.VMEM((heads, tokens, dim), BF16),
            pltpu.VMEM((heads, tokens, dim), BF16),
            pltpu.VMEM((heads, dim, dim), F32),
            pltpu.VMEM((heads, dim, dim), BF16),
            pltpu.VMEM((heads // 2, dim, dim), F32),
            pltpu.VMEM((heads // 2, dim, dim), BF16),
            pltpu.VMEM((quarter, dim, dim), F32),
            pltpu.VMEM((bits - 2, quarter, dim, dim), BF16),
            pltpu.VMEM((bits, heads, dim, dim), BF16),
            pltpu.VMEM((heads, tokens, dim), F32),
            pltpu.VMEM((heads, tokens, 8), F32),
            pltpu.SemaphoreType.DMA((3,)),
            pltpu.SemaphoreType.DMA((copies,)),
            pltpu.SemaphoreType.DMA((copies,)),
        ],
        compiler_params=pltpu.CompilerParams(
            collective_id=0, has_side_effects=True, vmem_limit_bytes=56 * 2**20
        ),
    )(
        query_rows, key_rows, value_rows, conv_taps, level_table,
        table_index.reshape(1, tokens), level_columns,
    )


def solution(mesh):
    rows = P(("groups", "ctx"), None)
    return jax.shard_map(
        on_device,
        mesh=mesh,
        in_specs=(rows, rows, rows, P(), P(), P(("groups", "ctx")), rows),
        out_specs=rows,
        check_vma=False,
    )
```

profile of v0, /device:TPU:27, one launch (start us, length us, event | category | flops | bytes accessed | tf_op | source)
XLA Modules:
  0.0 72.5 jit_solution(8241828649420123026)
XLA Ops:
  0.0 2.0 %copy.8.table_ref = f32[64,12,32]{2,1,0:T(8,128)} copy(f32[64,12,32]{0,2,1:T(8,128)} %param.11) | data formatting | bytes 196608 | tf_op args[4]
  2.0 67.4 %shard_map.73 = bf16[256,4096]{1,0:T(8,128)(2,1)} custom-call(bf16[256,4096]{1,0:T(8,128)(2,1)} %q_hbm.1, bf16[256,4096]{1,0:T(8,128)(2,1)} %k_hbm.1, bf16[256,4096]{1,0:T(8,128)(2,1)} %v_hbm.1, f32[2,4,4096]{2,1,0:T(4,128)} %taps_ref.1, f32[64,12,32]{2,1,0:T(8,128)} %copy.8.table_ref, s32[1,256]{1,0:T(1,128)} %bitcast.1, s32[1,12]{1,0:T(1,128)} %cols_ref.1), custom_call_target="tpu_custom_call" | custom-call | tf_op jit(solution)/shard_map/pallas_call | solution.py:310
  69.3 3.1 %copy.10 = bf16[256,4096]{1,0:T(8,128)(2,1)} copy(bf16[256,4096]{1,0:T(8,128)(2,1)} %shard_map.73) | data formatting | bytes 4194304
where the time goes:
time: 72.7 us; the launch traced here: 72.5 us
  Pallas kernels  67.4 us (93%)
  local copies, waits for them, and re-layouts  5.1 us (7%)
    pallas_call x1, Pallas kernels, on_device(): pl.pallas_call(functools.partial(kernel, bits, heads, dim), out_shape=jax...  67.4 us
    unnamed x2, local copies, waits for them, and re-layouts  5.1 us

commit v1 on v0

--- a/solution.py
+++ b/solution.py
@@ -109,21 +109,52 @@
             total = total + taps[count - 1 - back : count - back] * pltpu.roll(rows, back, 0)[PAD:]
         return (0.5 * total * (1.0 + jnp.tanh(0.5 * total))).astype(BF16)
 
-    def state_body(h, carry):
+    def loop(first, count, step, one):
+        def body(i, carry):
+            stores = [one(first + i * step + u) for u in range(step)]
+            for group_of in stores:
+                for ref, at, value in group_of:
+                    ref[at] = value
+            return carry
+
+        lax.fori_loop(0, count // step, body, 0)
+
+    def state_one(h):
         key = conv(k_v, 1, h)
-        kc[h] = key
         state = lax.dot_general(
             key, v_v[:, lanes(h)], (((0,), (0,)), ((), ())), preferred_element_type=F32
         )
-        st_f[h] = state
-        st_b[h] = state.astype(BF16)
-        return carry
+        return (kc, h, key), (st_f, h, state), (st_b, h, state.astype(BF16))
 
     own_half = bit[0] * half
     other_half = (1 - bit[0]) * half
     own_quart = own_half + bit[1] * quarter
     other_quart = own_half + (1 - bit[1]) * quarter
 
+    def coefficients():
+        table = table_ref[...]
+        levels, _, rows = table.shape
+        factors = level_factors(levels, tokens, dim)
+        head_id = lax.broadcasted_iota(jnp.int32, (heads * 8, heads), 1)
+        lane_id = lax.broadcasted_iota(jnp.int32, (heads * 8, heads), 0)
+        leading = lax.broadcasted_iota(jnp.int32, table.shape, 0)
+        mixed = jnp.zeros((heads * 8, rows), F32)
+        for level in range(bits + 1):
+            column = jnp.sum(jnp.where(leading == cols_ref[0, level], table, 0.0), axis=0)
+            place = (lane_id == head_id * 8 + level).astype(F32)
+            mixed = mixed + jnp.dot(
+                place, column * factors[level],
+                precision=lax.Precision.HIGHEST, preferred_element_type=F32,
+            )
+        hot = (lax.broadcasted_iota(jnp.int32, (rows, tokens), 0) == index_ref[...]).astype(F32)
+        weights = lax.dot_general(
+            hot.T, mixed, (((1,), (1,)), ((), ())),
+            precision=lax.Precision.HIGHEST, preferred_element_type=F32,
+        )
+        for h in range(heads):
+            coef[h] = weights[:, h * 8 : h * 8 + 8]
+
+    coefficients()
     loads[0].wait()
     loads[1].wait()
     finish_rim(0, k_v)
@@ -132,35 +163,11 @@
     ]
     pair = []
     for i, first in enumerate(firsts):
-        lax.fori_loop(first, first + quarter, state_body, 0)
+        loop(first, quarter, 2, state_one)
         heads_i = pl.ds(first, quarter)
         copy = remote(2 + i, st_b.at[heads_i], buck.at[0, heads_i], partner[0])
         send(copy, None if i < 2 else bit[0] == 0)
         pair.append(copy)
-
-    def coefficients():
-        table = table_ref[...]
-        rows, levels, _ = table.shape
-        factors = level_factors(levels, tokens, dim)
-        middle = lax.broadcasted_iota(jnp.int32, table.shape, 1)
-        head_id = lax.broadcasted_iota(jnp.int32, (heads, heads * 8), 0)
-        lane_id = lax.broadcasted_iota(jnp.int32, (heads, heads * 8), 1)
-        mixed = jnp.zeros((rows, heads * 8), F32)
-        for level in range(bits + 1):
-            column = jnp.sum(jnp.where(middle == cols_ref[0, level], table, 0.0), axis=1)
-            place = (lane_id == head_id * 8 + level).astype(F32)
-            mixed = mixed + jnp.dot(
-                column * factors[level], place,
-                precision=lax.Precision.HIGHEST, preferred_element_type=F32,
-            )
-        hot = (lax.broadcasted_iota(jnp.int32, (rows, tokens), 0) == index_ref[...]).astype(F32)
-        weights = jnp.dot(
-            hot.T, mixed, precision=lax.Precision.HIGHEST, preferred_element_type=F32
-        )
-        for h in range(heads):
-            coef[h] = weights[:, h * 8 : h * 8 + 8]
-
-    coefficients()
 
     for i in range(2):
         wait(pair[i])
@@ -187,23 +194,22 @@
         jnp.int32, (tokens, tokens), 1
     )
 
-    def local_body(h, carry):
+    def local_one(h):
         query = conv(q_v, 0, h)
-        qc[h] = query
         score = lax.dot_general(
             query, kc[h], (((1,), (1,)), ((), ())), preferred_element_type=F32
         )
         score = jnp.where(causal, score, 0.0).astype(BF16)
         read = jnp.dot(score, v_v[:, lanes(h)], preferred_element_type=F32)
-        acc[h] = read * coef[h][:, 0:1]
-        return carry
+        return (qc, h, query), (acc, h, read * coef[h][:, 0:1])
 
     def local(part):
-        lax.fori_loop(part * quarter, (part + 1) * quarter, local_body, 0)
+        loop(part * quarter, quarter, 2, local_one)
 
     loads[2].wait()
     finish_rim(1, q_v)
     local(0)
+    local(1)
 
     wait(shares[0])
 
@@ -218,7 +224,7 @@
 
     def exchange(b):
         copy = remote(
-            base + 3 * (b - 2), quart_b.at[b - 2], buck.at[b, pl.ds(own_quart, quarter)], partner[b]
+            base + 4 * (b - 2), quart_b.at[b - 2], buck.at[b, pl.ds(own_quart, quarter)], partner[b]
         )
         send(copy, None if b < bits - 1 else bit[b] == 0)
         return copy
@@ -230,26 +236,36 @@
         8, buck.at[1, pl.ds(own_half, half)], buck.at[1, pl.ds(own_half, half)], partner[0]
     )
     send(over, bit[1] == 1)
-    local(1)
+    local(2)
+    local(3)
 
     def gather_x(b):
         quart = buck.at[b, pl.ds(own_quart, quarter)]
-        copy = remote(base + 3 * (b - 2) + 1, quart, quart, partner[1])
+        copy = remote(base + 4 * (b - 2) + 1, quart, quart, partner[1])
         send(copy, bit[b] == 1)
         return copy
 
-    def gather_core(b):
-        own = buck.at[b, pl.ds(own_half, half)]
-        copy = remote(base + 3 * (b - 2) + 2, own, own, partner[0])
+    def gather_core(b, i, first):
+        quart = buck.at[b, pl.ds(first, quarter)]
+        copy = remote(base + 4 * (b - 2) + 2 + i, quart, quart, partner[0])
         send(copy, bit[b] == 1)
         return copy
 
-    gx = {}
-    gc = {}
+    def level_term(b, h):
+        read = jnp.dot(qc[h], buck[b, h], preferred_element_type=F32)
+        return acc[h] + read * coef[h][:, b + 1 : b + 2]
+
+    def read_level(b):
+        @pl.when(bit[b] == 1)
+        def _():
+            loop(0, heads, 4, lambda h: ((acc, h, level_term(b, h)),))
+
+    last = bits - 1
     for b in range(2, bits):
-        wait(hops[b], None if b < bits - 1 else bit[b] == 1)
-        gx[b] = gather_x(b)
-        if b < bits - 1:
+        wait(hops[b], None if b < last else bit[b] == 1)
+        across = gather_x(b)
+        near = gather_core(b, 0, own_quart)
+        if b < last:
 
             def more_body(i, carry, b=b):
                 total = quart_f[i] + buck[b, own_quart + i].astype(F32)
@@ -259,37 +275,45 @@
 
             lax.fori_loop(0, quarter, more_body, 0)
             hops[b + 1] = exchange(b + 1)
-        if b == 2:
-            local(2)
-            local(3)
-        wait(gx[b], bit[b] == 1)
-        gc[b] = gather_core(b)
-
-    def read_level(b):
-        def body(h, carry):
-            acc[h] += (
-                jnp.dot(qc[h], buck[b, h], preferred_element_type=F32) * coef[h][:, b + 1 : b + 2]
-            )
-            return carry
-
-        @pl.when(bit[b] == 1)
-        def _():
-            lax.fori_loop(0, heads, body, 0)
-
-    wait(pair[2], bit[0] == 1)
-    wait(pair[3], bit[0] == 1)
-    read_level(0)
-    wait(over, bit[1] == 1)
-    read_level(1)
-    for b in range(2, bits):
-        wait(gc[b], bit[b] == 1)
-        read_level(b)
-
-    def out_body(h, carry):
-        out_ref[:, lanes(h)] = acc[h].astype(BF16)
-        return carry
-
-    lax.fori_loop(0, heads, out_body, 0)
+            if b == 2:
+                wait(pair[2], bit[0] == 1)
+                wait(pair[3], bit[0] == 1)
+                read_level(0)
+                wait(over, bit[1] == 1)
+                read_level(1)
+            wait(across, bit[b] == 1)
+            far = gather_core(b, 1, other_quart)
+            wait(near, bit[b] == 1)
+            wait(far, bit[b] == 1)
+            read_level(b)
+
+    def finish(first):
+        def out_at(h):
+            return (slice(None), lanes(h))
+
+        loop(
+            first, quarter, 4,
+            lambda h: ((out_ref, out_at(h), level_term(last, h).astype(BF16)),),
+        )
+
+    @pl.when(bit[last] == 1)
+    def _():
+        finish(own_quart)
+        near.wait_recv()
+        finish(other_half + bit[1] * quarter)
+        across.wait_recv()
+
+    far = gather_core(last, 1, other_quart)
+
+    @pl.when(bit[last] == 1)
+    def _():
+        finish(other_quart)
+        far.wait_recv()
+        finish(other_half + (1 - bit[1]) * quarter)
+
+    @pl.when(bit[last] == 0)
+    def _():
+        loop(0, heads, 4, lambda h: ((out_ref, (slice(None), lanes(h)), acc[h].astype(BF16)),))
 
     for copy, when in started:
         if when is None:
@@ -306,7 +330,7 @@
     quarter = heads // 4
     vmem = pl.BlockSpec(memory_space=pltpu.VMEM)
     hbm = pl.BlockSpec(memory_space=pl.ANY)
-    copies = 9 + 3 * (bits - 2)
+    copies = 9 + 4 * (bits - 2)
     return pl.pallas_call(
         functools.partial(kernel, bits, heads, dim),
         out_shape=jax.ShapeDtypeStruct((tokens, width), BF16),
@@ -335,7 +359,7 @@
             collective_id=0, has_side_effects=True, vmem_limit_bytes=56 * 2**20
         ),
     )(
-        query_rows, key_rows, value_rows, conv_taps, level_table,
+        query_rows, key_rows, value_rows, conv_taps, level_table.transpose(1, 2, 0),
         table_index.reshape(1, tokens), level_columns,
     )
 

time: 72.7 us -> 53.3 us (0.73)
  the two profiles are of different devices: /device:TPU:27 before, /device:TPU:25 now
where the time goes in v1:
time: 53.3 us; the launch traced here: 53.1 us
  Pallas kernels  50 us (94%)
  local copies, waits for them, and re-layouts  3.13 us (6%)
    pallas_call x1, Pallas kernels, on_device(): pl.pallas_call(functools.partial(kernel, bits, heads, dim), out_shape=jax...  50 us
    unnamed x1, local copies, waits for them, and re-layouts  3.13 us

profile of v1, /device:TPU:25, one launch (start us, length us, event | category | flops | bytes accessed | tf_op | source)
XLA Modules:
  0.0 53.1 jit_solution(128551468661477262)
XLA Ops:
  0.0 50.0 %shard_map.73 = bf16[256,4096]{1,0:T(8,128)(2,1)} custom-call(bf16[256,4096]{1,0:T(8,128)(2,1)} %q_hbm.1, bf16[256,4096]{1,0:T(8,128)(2,1)} %k_hbm.1, bf16[256,4096]{1,0:T(8,128)(2,1)} %v_hbm.1, f32[2,4,4096]{2,1,0:T(4,128)} %taps_ref.1, f32[12,32,64]{2,1,0:T(8,128)} %bitcast.2, s32[1,256]{1,0:T(1,128)} %bitcast.3, s32[1,12]{1,0:T(1,128)} %cols_ref.1), custom_call_target="tpu_custom_call" | custom-call | tf_op jit(solution)/shard_map/pallas_call | solution.py:334
  50.0 3.1 %copy.9 = bf16[256,4096]{1,0:T(8,128)(2,1)} copy(bf16[256,4096]{1,0:T(8,128)(2,1)} %shard_map.73) | data formatting | bytes 4194304

commit v2 on v1

--- a/solution.py
+++ b/solution.py
@@ -34,6 +34,7 @@
     partner = [pos + 2**b * (1 - 2 * bit[b]) for b in range(bits)]
     quarter = heads // 4
     half = heads // 2
+    piece = quarter // 2
 
     loads = [
         pltpu.make_async_copy(src, dst.at[pl.ds(start, tokens)], load_sem.at[i])
@@ -181,13 +182,15 @@
 
     lax.fori_loop(0, half, half_body, 0)
     shares = []
-    for i, (inner, first) in enumerate((
-        ((1 - bit[1]) * quarter, other_quart), (bit[1] * quarter, own_quart)
+    for i, (inner, first, count, when) in enumerate((
+        ((1 - bit[1]) * quarter, other_quart, piece, None),
+        ((1 - bit[1]) * quarter + piece, other_quart + piece, piece, None),
+        (bit[1] * quarter, own_quart, quarter, bit[1] == 0),
     )):
         copy = remote(
-            6 + i, half_b.at[pl.ds(inner, quarter)], buck.at[1, pl.ds(first, quarter)], partner[1]
-        )
-        send(copy, None if i == 0 else bit[1] == 0)
+            6 + i, half_b.at[pl.ds(inner, count)], buck.at[1, pl.ds(first, count)], partner[1]
+        )
+        send(copy, when)
         shares.append(copy)
 
     causal = lax.broadcasted_iota(jnp.int32, (tokens, tokens), 0) >= lax.broadcasted_iota(
@@ -208,48 +211,50 @@
 
     loads[2].wait()
     finish_rim(1, q_v)
+    base = 10
+
+    def stage(b, i, part, ref_from, first, other, when):
+        copy = remote(
+            base + 8 * (b - 2) + 2 * i + part,
+            ref_from, buck.at[b, pl.ds(first + part * piece, piece)], other,
+        )
+        send(copy, when)
+        return copy
+
+    def exchange(b, part):
+        return stage(
+            b, 0, part, quart_b.at[b - 2, pl.ds(part * piece, piece)], own_quart,
+            partner[b], None if b < last else bit[b] == 0,
+        )
+
+    def pass_on(b, i, part, first, other):
+        here = buck.at[b, pl.ds(first + part * piece, piece)]
+        return stage(b, i, part, here, first, other, bit[b] == 1)
+
+    last = bits - 1
+
+    def plane(part):
+        def body(i, carry):
+            total = half_f[bit[1] * quarter + i] + buck[1, own_quart + i].astype(F32)
+            quart_f[i] = total
+            quart_b[0, i] = total.astype(BF16)
+            return carry
+
+        wait(shares[part])
+        lax.fori_loop(part * piece, (part + 1) * piece, body, 0)
+        return exchange(2, part)
+
     local(0)
+    first_hop = plane(0)
     local(1)
-
-    wait(shares[0])
-
-    def quart_body(i, carry):
-        total = half_f[bit[1] * quarter + i] + buck[1, own_quart + i].astype(F32)
-        quart_f[i] = total
-        quart_b[0, i] = total.astype(BF16)
-        return carry
-
-    lax.fori_loop(0, quarter, quart_body, 0)
-    base = 9
-
-    def exchange(b):
-        copy = remote(
-            base + 4 * (b - 2), quart_b.at[b - 2], buck.at[b, pl.ds(own_quart, quarter)], partner[b]
-        )
-        send(copy, None if b < bits - 1 else bit[b] == 0)
-        return copy
-
-    hops = {2: exchange(2)}
-
-    wait(shares[1], bit[1] == 1)
+    hops = {2: [first_hop, plane(1)]}
+
+    wait(shares[2], bit[1] == 1)
     over = remote(
-        8, buck.at[1, pl.ds(own_half, half)], buck.at[1, pl.ds(own_half, half)], partner[0]
+        9, buck.at[1, pl.ds(own_half, half)], buck.at[1, pl.ds(own_half, half)], partner[0]
     )
     send(over, bit[1] == 1)
     local(2)
-    local(3)
-
-    def gather_x(b):
-        quart = buck.at[b, pl.ds(own_quart, quarter)]
-        copy = remote(base + 4 * (b - 2) + 1, quart, quart, partner[1])
-        send(copy, bit[b] == 1)
-        return copy
-
-    def gather_core(b, i, first):
-        quart = buck.at[b, pl.ds(first, quarter)]
-        copy = remote(base + 4 * (b - 2) + 2 + i, quart, quart, partner[0])
-        send(copy, bit[b] == 1)
-        return copy
 
     def level_term(b, h):
         read = jnp.dot(qc[h], buck[b, h], preferred_element_type=F32)
@@ -260,12 +265,10 @@
         def _():
             loop(0, heads, 4, lambda h: ((acc, h, level_term(b, h)),))
 
-    last = bits - 1
-    for b in range(2, bits):
-        wait(hops[b], None if b < last else bit[b] == 1)
-        across = gather_x(b)
-        near = gather_core(b, 0, own_quart)
-        if b < last:
+    for b in range(2, last):
+        across, near, far, onward = [], [], [], []
+        for part in range(2):
+            wait(hops[b][part])
 
             def more_body(i, carry, b=b):
                 total = quart_f[i] + buck[b, own_quart + i].astype(F32)
@@ -273,43 +276,57 @@
                 quart_b[b - 1, i] = total.astype(BF16)
                 return carry
 
-            lax.fori_loop(0, quarter, more_body, 0)
-            hops[b + 1] = exchange(b + 1)
-            if b == 2:
-                wait(pair[2], bit[0] == 1)
-                wait(pair[3], bit[0] == 1)
-                read_level(0)
-                wait(over, bit[1] == 1)
-                read_level(1)
-            wait(across, bit[b] == 1)
-            far = gather_core(b, 1, other_quart)
-            wait(near, bit[b] == 1)
-            wait(far, bit[b] == 1)
-            read_level(b)
+            lax.fori_loop(part * piece, (part + 1) * piece, more_body, 0)
+            onward.append(exchange(b + 1, part))
+            across.append(pass_on(b, 1, part, own_quart, partner[1]))
+            near.append(pass_on(b, 2, part, own_quart, partner[0]))
+            if b == 2 and part == 0:
+                local(3)
+        hops[b + 1] = onward
+        if b == 2:
+            wait(pair[2], bit[0] == 1)
+            wait(pair[3], bit[0] == 1)
+            read_level(0)
+        for part in range(2):
+            wait(across[part], bit[b] == 1)
+            far.append(pass_on(b, 3, part, other_quart, partner[0]))
+        if b == 2:
+            wait(over, bit[1] == 1)
+            read_level(1)
+        for copy in near + far:
+            wait(copy, bit[b] == 1)
+        read_level(b)
 
     def finish(first):
-        def out_at(h):
-            return (slice(None), lanes(h))
-
-        loop(
-            first, quarter, 4,
-            lambda h: ((out_ref, out_at(h), level_term(last, h).astype(BF16)),),
-        )
-
-    @pl.when(bit[last] == 1)
-    def _():
-        finish(own_quart)
-        near.wait_recv()
-        finish(other_half + bit[1] * quarter)
-        across.wait_recv()
-
-    far = gather_core(last, 1, other_quart)
-
-    @pl.when(bit[last] == 1)
-    def _():
-        finish(other_quart)
-        far.wait_recv()
-        finish(other_half + (1 - bit[1]) * quarter)
+        @pl.when(bit[last] == 1)
+        def _():
+            loop(
+                first, piece, 4,
+                lambda h: (
+                    (out_ref, (slice(None), lanes(h)), level_term(last, h).astype(BF16)),
+                ),
+            )
+
+    across, near, far = [], [], []
+    near_quart = other_half + bit[1] * quarter
+    far_quart = other_half + (1 - bit[1]) * quarter
+    for part in range(2):
+        wait(hops[last][part], bit[last] == 1)
+        across.append(pass_on(last, 1, part, own_quart, partner[1]))
+        near.append(pass_on(last, 2, part, own_quart, partner[0]))
+        finish(own_quart + part * piece)
+    wait(near[0], bit[last] == 1)
+    finish(near_quart)
+    for part in range(2):
+        wait(across[part], bit[last] == 1)
+        far.append(pass_on(last, 3, part, other_quart, partner[0]))
+        finish(other_quart + part * piece)
+        if part == 0:
+            wait(near[1], bit[last] == 1)
+            finish(near_quart + piece)
+    for part in range(2):
+        wait(far[part], bit[last] == 1)
+        finish(far_quart + part * piece)
 
     @pl.when(bit[last] == 0)
     def _():
@@ -330,7 +347,7 @@
     quarter = heads // 4
     vmem = pl.BlockSpec(memory_space=pltpu.VMEM)
     hbm = pl.BlockSpec(memory_space=pl.ANY)
-    copies = 9 + 4 * (bits - 2)
+    copies = 10 + 8 * (bits - 2)
     return pl.pallas_call(
         functools.partial(kernel, bits, heads, dim),
         out_shape=jax.ShapeDtypeStruct((tokens, width), BF16),

time: 53.3 us -> 50.7 us (0.951)
  the two profiles are of different devices: /device:TPU:25 before, /device:TPU:27 now
where the time goes in v2:
time: 50.7 us; the launch traced here: 50.5 us
  Pallas kernels  47.3 us (93%)
  local copies, waits for them, and re-layouts  3.13 us (6%)
    pallas_call x1, Pallas kernels, on_device(): pl.pallas_call(functools.partial(kernel, bits, heads, dim), out_shape=jax...  47.3 us
    unnamed x1, local copies, waits for them, and re-layouts  3.13 us

profile of v2, /device:TPU:27, one launch (start us, length us, event | category | flops | bytes accessed | tf_op | source)
XLA Modules:
  0.0 50.5 jit_solution(13672472544572682880)
XLA Ops:
  0.0 47.3 %shard_map.73 = bf16[256,4096]{1,0:T(8,128)(2,1)} custom-call(bf16[256,4096]{1,0:T(8,128)(2,1)} %q_hbm.1, bf16[256,4096]{1,0:T(8,128)(2,1)} %k_hbm.1, bf16[256,4096]{1,0:T(8,128)(2,1)} %v_hbm.1, f32[2,4,4096]{2,1,0:T(4,128)} %taps_ref.1, f32[12,32,64]{2,1,0:T(8,128)} %bitcast.2, s32[1,256]{1,0:T(1,128)} %bitcast.3, s32[1,12]{1,0:T(1,128)} %cols_ref.1), custom_call_target="tpu_custom_call" | custom-call | tf_op jit(solution)/shard_map/pallas_call | solution.py:351
  47.4 3.1 %copy.9 = bf16[256,4096]{1,0:T(8,128)(2,1)} copy(bf16[256,4096]{1,0:T(8,128)(2,1)} %shard_map.73) | data formatting | bytes 4194304

commit v3 on v2

--- a/solution.py
+++ b/solution.py
@@ -164,7 +164,7 @@
     ]
     pair = []
     for i, first in enumerate(firsts):
-        loop(first, quarter, 2, state_one)
+        loop(first, quarter, 4, state_one)
         heads_i = pl.ds(first, quarter)
         copy = remote(2 + i, st_b.at[heads_i], buck.at[0, heads_i], partner[0])
         send(copy, None if i < 2 else bit[0] == 0)
@@ -207,7 +207,7 @@
         return (qc, h, query), (acc, h, read * coef[h][:, 0:1])
 
     def local(part):
-        loop(part * quarter, quarter, 2, local_one)
+        loop(part * quarter, quarter, 4, local_one)
 
     loads[2].wait()
     finish_rim(1, q_v)

time: 50.7 us -> 47.6 us (0.939)
  Pallas kernels: 47.3 us -> 44.3 us
    pallas_call x1, Pallas kernels: 47.3 us -> 44.3 us  [on_device(): pl.pallas_call(functools.partial(kernel, bits, heads, dim), out_shape=jax...]
where the time goes in v3:
time: 47.6 us; the launch traced here: 47.4 us
  Pallas kernels  44.3 us (93%)
  local copies, waits for them, and re-layouts  3.13 us (7%)
    pallas_call x1, Pallas kernels, on_device(): pl.pallas_call(functools.partial(kernel, bits, heads, dim), out_shape=jax...  44.3 us
    unnamed x1, local copies, waits for them, and re-layouts  3.13 us

profile of v3, /device:TPU:27, one launch (start us, length us, event | category | flops | bytes accessed | tf_op | source)
XLA Modules:
  0.0 47.4 jit_solution(10894003852278255070)
XLA Ops:
  0.0 44.3 %shard_map.73 = bf16[256,4096]{1,0:T(8,128)(2,1)} custom-call(bf16[256,4096]{1,0:T(8,128)(2,1)} %q_hbm.1, bf16[256,4096]{1,0:T(8,128)(2,1)} %k_hbm.1, bf16[256,4096]{1,0:T(8,128)(2,1)} %v_hbm.1, f32[2,4,4096]{2,1,0:T(4,128)} %taps_ref.1, f32[12,32,64]{2,1,0:T(8,128)} %bitcast.2, s32[1,256]{1,0:T(1,128)} %bitcast.3, s32[1,12]{1,0:T(1,128)} %cols_ref.1), custom_call_target="tpu_custom_call" | custom-call | tf_op jit(solution)/shard_map/pallas_call | solution.py:351
  44.3 3.1 %copy.9 = bf16[256,4096]{1,0:T(8,128)(2,1)} copy(bf16[256,4096]{1,0:T(8,128)(2,1)} %shard_map.73) | data formatting | bytes 4194304

commit v4 on v3

--- a/solution.py
+++ b/solution.py
@@ -163,15 +163,13 @@
         other_half + (1 - bit[1]) * quarter, other_half + bit[1] * quarter, other_quart, own_quart
     ]
     pair = []
-    for i, first in enumerate(firsts):
-        loop(first, quarter, 4, state_one)
-        heads_i = pl.ds(first, quarter)
+
+    def states(i):
+        loop(firsts[i], quarter, 4, state_one)
+        heads_i = pl.ds(firsts[i], quarter)
         copy = remote(2 + i, st_b.at[heads_i], buck.at[0, heads_i], partner[0])
         send(copy, None if i < 2 else bit[0] == 0)
         pair.append(copy)
-
-    for i in range(2):
-        wait(pair[i])
 
     def half_body(i, carry):
         h = own_half + i
@@ -180,18 +178,30 @@
         half_b[i] = total.astype(BF16)
         return carry
 
-    lax.fori_loop(0, half, half_body, 0)
     shares = []
-    for i, (inner, first, count, when) in enumerate((
-        ((1 - bit[1]) * quarter, other_quart, piece, None),
-        ((1 - bit[1]) * quarter + piece, other_quart + piece, piece, None),
-        (bit[1] * quarter, own_quart, quarter, bit[1] == 0),
-    )):
+
+    def share(inner, first, count, when):
         copy = remote(
-            6 + i, half_b.at[pl.ds(inner, count)], buck.at[1, pl.ds(first, count)], partner[1]
+            6 + len(shares), half_b.at[pl.ds(inner, count)],
+            buck.at[1, pl.ds(first, count)], partner[1],
         )
         send(copy, when)
         shares.append(copy)
+
+    states(0)
+    states(1)
+    states(2)
+    wait(pair[0])
+    inner = (1 - bit[1]) * quarter
+    for part in range(2):
+        start = inner + part * piece
+        lax.fori_loop(start, start + piece, half_body, 0)
+        share(start, own_half + start, piece, None)
+    states(3)
+    wait(pair[1])
+    inner = bit[1] * quarter
+    lax.fori_loop(inner, inner + quarter, half_body, 0)
+    share(inner, own_quart, quarter, bit[1] == 0)
 
     causal = lax.broadcasted_iota(jnp.int32, (tokens, tokens), 0) >= lax.broadcasted_iota(
         jnp.int32, (tokens, tokens), 1

time: 47.6 us -> 46.3 us (0.973)
  Pallas kernels: 44.3 us -> 43 us
    pallas_call x1, Pallas kernels: 44.3 us -> 43 us  [on_device(): pl.pallas_call(functools.partial(kernel, bits, heads, dim), out_shape=jax...]
where the time goes in v4:
time: 46.3 us; the launch traced here: 46.2 us
  Pallas kernels  43 us (93%)
  local copies, waits for them, and re-layouts  3.13 us (7%)
    pallas_call x1, Pallas kernels, on_device(): pl.pallas_call(functools.partial(kernel, bits, heads, dim), out_shape=jax...  43 us
    unnamed x1, local copies, waits for them, and re-layouts  3.13 us

profile of v4, /device:TPU:27, one launch (start us, length us, event | category | flops | bytes accessed | tf_op | source)
XLA Modules:
  0.0 46.2 jit_solution(9902982712926071631)
XLA Ops:
  0.0 43.0 %shard_map.73 = bf16[256,4096]{1,0:T(8,128)(2,1)} custom-call(bf16[256,4096]{1,0:T(8,128)(2,1)} %q_hbm.1, bf16[256,4096]{1,0:T(8,128)(2,1)} %k_hbm.1, bf16[256,4096]{1,0:T(8,128)(2,1)} %v_hbm.1, f32[2,4,4096]{2,1,0:T(4,128)} %taps_ref.1, f32[12,32,64]{2,1,0:T(8,128)} %bitcast.2, s32[1,256]{1,0:T(1,128)} %bitcast.3, s32[1,12]{1,0:T(1,128)} %cols_ref.1), custom_call_target="tpu_custom_call" | custom-call | tf_op jit(solution)/shard_map/pallas_call | solution.py:361
  43.1 3.1 %copy.9 = bf16[256,4096]{1,0:T(8,128)(2,1)} copy(bf16[256,4096]{1,0:T(8,128)(2,1)} %shard_map.73) | data formatting | bytes 4194304
